TPU v7x, 32 devices: a whole 2x2x4 slice. The times are simulated.
32 devices in a mesh: pipe: 4 (over z), blk: 2 (over x), uly: 4 (over y, core).
Axes of the slice: x: 2, y: 2, z: 4, core: 2. Of those that a mesh axis runs over, the one named last changes fastest.
Arguments:
- hidden_in: bfloat16 [4, 64, 3072], P('pipe', ('blk', 'uly')), may hold values from -6 to 6
- text_len: int32 [1], replicated, may hold values from 16 to 64
- qkv_video: bfloat16 [4, 3072, 3, 1536], P('pipe', 'blk', None, 'uly'), may hold values from -0.109375 to 0.109375
- qkv_text: bfloat16 [2, 3072, 3, 1536], P(None, 'blk', None, 'uly'), may hold values from -0.109375 to 0.109375
- out_video: bfloat16 [4, 1536, 3072], P('pipe', 'uly', 'blk'), may hold values from -0.15625 to 0.15625
- out_text: bfloat16 [2, 1536, 3072], P(None, 'uly', 'blk'), may hold values from -0.15625 to 0.15625
- modulation: float32 [4, 2, 3, 3072], P('pipe'), may hold values from -3 to 3
- qk_gain: float32 [4, 2, 2, 128], P('pipe'), may hold values from 1 to 3
- stale_kv: bfloat16 [4, 2, 256, 1536], P('pipe', None, None, 'uly'), may hold values from -24 to 24, as said below
Outputs:
- hidden_out: bfloat16 [4, 64, 3072], P('pipe', ('blk', 'uly'))
Inputs may be any that keep to these rules, and one draw needn't show every extreme that they name: `stale_kv`: stale keys and values of order one, some keys larger.
All inputs are finite; a program needn't handle non-finite values.
Results may differ from a plain program's by a relative error of at most 0.04.
Values may be sent and summed in bfloat16 or wider, within the bound.
A program may use at most 128 MiB of HBM per device.

v0:
```python
import math
import jax
import jax.numpy as jnp
from jax import lax
from jax.sharding import PartitionSpec as P


def from_behind(shard, axis, by):
    size = lax.axis_size(axis)
    pairs = [(i, i + by) for i in range(size) if 0 <= i + by < size]
    return lax.ppermute(shard, axis, pairs)


def rms_scale(values, gain):
    squares = jnp.mean(values * values, axis=-1, keepdims=True)
    return values * lax.rsqrt(squares + 1e-06) * gain


def local(
    hidden_in, text_len, qkv_video, qkv_text, out_video, out_text, modulation, qk_gain, stale_kv
):
    sections = lax.axis_size("pipe")
    blk_count = lax.axis_size("blk")
    uly_count = lax.axis_size("uly")
    section = lax.axis_index("pipe")
    blk_index = lax.axis_index("blk")
    rows = hidden_in.shape[1]
    width = hidden_in.shape[2]
    group = rows * uly_count
    micro = group * blk_count
    text_count = 2 * group
    dual_count = qkv_text.shape[0]
    head_dim = qk_gain.shape[3]
    local_width = stale_kv.shape[3]
    local_heads = local_width // head_dim
    inv_scale = 1.0 / math.sqrt(head_dim)
    dual = section < dual_count
    chosen = jnp.minimum(section, dual_count - 1)
    text_rows_w = lax.dynamic_index_in_dim(qkv_text, chosen, 0, keepdims=False)
    text_cols_w = lax.dynamic_index_in_dim(out_text, chosen, 0, keepdims=False)
    video_proj, text_proj, video_back, text_back = (
        lax.all_gather(qkv_video[0], "blk", axis=0, tiled=True),
        lax.all_gather(text_rows_w, "blk", axis=0, tiled=True),
        lax.all_gather(out_video[0], "blk", axis=1, tiled=True),
        lax.all_gather(text_cols_w, "blk", axis=1, tiled=True),
    )
    video_proj = video_proj.reshape(width, 3 * local_width)
    text_proj = text_proj.reshape(width, 3 * local_width)
    mods = modulation[0]
    gains = qk_gain[0]
    stale = stale_kv[0]
    valid_text = text_len[0]
    cache_keys = stale[0]
    cache_values = stale[1]
    places = jnp.arange(micro * sections, dtype=jnp.int32)
    key_ok = (places >= text_count) | (places < valid_text)
    carried = jnp.zeros((rows, width), jnp.bfloat16)
    inbox = hidden_in[0]
    outbox = jnp.zeros((rows, width), jnp.bfloat16)
    last_tick = 2 * sections - 2
    for tick in range(2 * sections - 1):
        micro_index = tick - section
        valid = (micro_index >= 0) & (micro_index < sections)
        current = jnp.clip(micro_index, 0, sections - 1)
        entering = jnp.where(section == 0, inbox, carried)
        is_text = dual & (current * micro + blk_index * group < text_count)
        stream = is_text.astype(jnp.int32)
        mod_rows = lax.dynamic_index_in_dim(mods, stream, 0, keepdims=False)
        gain_rows = lax.dynamic_index_in_dim(gains, stream, 0, keepdims=False)
        floats = entering.astype(jnp.float32)
        centred = floats - jnp.mean(floats, axis=-1, keepdims=True)
        normed = centred * lax.rsqrt(jnp.mean(centred * centred, axis=-1, keepdims=True) + 1e-06)
        modded = (normed * (1.0 + mod_rows[1]) + mod_rows[0]).astype(jnp.bfloat16)
        gathered = lax.all_gather(modded, "uly", axis=0, tiled=True)
        projected = lax.cond(
            is_text,
            lambda operand: jnp.dot(operand, text_proj, preferred_element_type=jnp.float32),
            lambda operand: jnp.dot(operand, video_proj, preferred_element_type=jnp.float32),
            gathered,
        )
        projected = projected.reshape(group, 3, local_heads, head_dim)
        queries = rms_scale(projected[:, 0], gain_rows[0]).astype(jnp.bfloat16)
        fresh_keys = (
            rms_scale(projected[:, 1], gain_rows[1])
            .astype(jnp.bfloat16)
            .reshape(group, local_width)
        )
        fresh_values = projected[:, 2].astype(jnp.bfloat16).reshape(group, local_width)
        all_keys, all_values = (
            lax.all_gather(fresh_keys, "blk", axis=0, tiled=True),
            lax.all_gather(fresh_values, "blk", axis=0, tiled=True),
        )
        offset = current * micro
        old_keys = lax.dynamic_slice_in_dim(cache_keys, offset, micro, 0)
        old_values = lax.dynamic_slice_in_dim(cache_values, offset, micro, 0)
        cache_keys = lax.dynamic_update_slice_in_dim(
            cache_keys, jnp.where(valid, all_keys, old_keys), offset, 0
        )
        cache_values = lax.dynamic_update_slice_in_dim(
            cache_values, jnp.where(valid, all_values, old_values), offset, 0
        )
        key_heads = cache_keys.reshape(-1, local_heads, head_dim)
        value_heads = cache_values.reshape(-1, local_heads, head_dim)
        scores = (
            jnp.einsum("rhd,lhd->hrl", queries, key_heads, preferred_element_type=jnp.float32)
            * inv_scale
        )
        scores = jnp.where(key_ok[None, None, :], scores, -1e30)
        peak = jnp.max(scores, axis=-1, keepdims=True)
        weights = jnp.where(key_ok[None, None, :], jnp.exp(scores - peak), 0.0)
        total = jnp.sum(weights, axis=-1)
        mixed = jnp.einsum(
            "hrl,lhd->rhd",
            weights.astype(jnp.bfloat16),
            value_heads,
            preferred_element_type=jnp.float32,
        )
        attended = (
            (mixed / jnp.transpose(total)[:, :, None])
            .reshape(group, local_width)
            .astype(jnp.bfloat16)
        )
        partial_value = lax.cond(
            is_text,
            lambda operand: jnp.dot(operand, text_back, preferred_element_type=jnp.float32),
            lambda operand: jnp.dot(operand, video_back, preferred_element_type=jnp.float32),
            attended,
        )
        summed = lax.psum_scatter(partial_value, "uly", scatter_dimension=0, tiled=True)
        leaving = (floats + mod_rows[2] * summed).astype(jnp.bfloat16)
        outbox = jnp.where((section == sections - 1) & valid, leaving, outbox)
        if tick < last_tick:
            carried = from_behind(leaving, "pipe", 1)
            inbox, outbox = from_behind((inbox, outbox), "pipe", -1)
    return outbox[None]


def solution(mesh):
    return jax.shard_map(
        local,
        mesh=mesh,
        in_specs=(
            P("pipe", ("blk", "uly"), None),
            P(),
            P("pipe", "blk", None, "uly"),
            P(None, "blk", None, "uly"),
            P("pipe", "uly", "blk"),
            P(None, "uly", "blk"),
            P("pipe", None, None, None),
            P("pipe", None, None, None),
            P("pipe", None, None, "uly"),
        ),
        out_specs=P("pipe", ("blk", "uly"), None),
        check_vma=False,
    )
```

profile of v0, /device:TPU:0, one launch (start us, length us, event | category | flops | bytes accessed | tf_op | source)
XLA Modules:
  0.0 631.8 jit_solution(11148494798743195502)
XLA Ops:
  10.8 6.1 copy.199
  16.9 6.1 copy.109
  30.0 6.9 %all_gather.75 = bf16[32,3072]{1,0:T(8,128)(2,1)S(1)} all-gather(bf16[8,3072]{1,0:T(8,128)(2,1)S(1)} %fusion.97), channel_id=1, replica_groups=mesh['pipe'=4,'blk'=2,'uly'=4] {'uly'}, dimensions={0}, use_global_device_ids=true | all-gather | bytes 245760 | tf_op jit(solution)/shard_map/all_gather | solution.py:74
  36.9 72.1 %all-gather.11.cloned.1.call-done = bf16[1,3072,3,384]{1,3,2,0:T(8,128)(2,1)} async-done(((bf16[1,1536,3,384]{1,3,2,0:T(8,128)(2,1)}), bf16[1,3072,3,384]{1,3,2,0:T(8,128)(2,1)}) %all-gather.11.cloned.1.call-update) | async-done | bytes 7077904 | tf_op jit(solution)/shard_map/all_gather | solution.py:43
  109.0 90.8 %all-gather.9.cloned.1.call-done = bf16[1,3072,3,384]{1,3,2,0:T(8,128)(2,1)} async-done(((bf16[1,1536,3,384]{1,3,2,0:T(8,128)(2,1)}), bf16[1,3072,3,384]{1,3,2,0:T(8,128)(2,1)}) %all-gather.9.cloned.1.call-update) | async-done | bytes 7077904 | tf_op jit(solution)/shard_map/all_gather | solution.py:42
  199.8 5.2 conditional.14
  199.8 5.2 fusion.171
  205.3 4.5 all_gather.79
  209.9 5.0 all_gather.78
  216.8 21.1 %all-gather.15.cloned.1.call-done = bf16[1,384,3072]{2,1,0:T(8,128)(2,1)} async-done(((bf16[1,384,1536]{2,1,0:T(8,128)(2,1)}), bf16[1,384,3072]{2,1,0:T(8,128)(2,1)}) %all-gather.15.cloned.1.call-update) | async-done | bytes 2359312 | tf_op jit(solution)/shard_map/all_gather | solution.py:45
  237.9 37.5 %all-gather.13.cloned.1.call-done = bf16[1,384,3072]{2,1,0:T(8,128)(2,1)} async-done(((bf16[1,384,1536]{2,1,0:T(8,128)(2,1)}), bf16[1,384,3072]{2,1,0:T(8,128)(2,1)}) %all-gather.13.cloned.1.call-update) | async-done | bytes 2359312 | tf_op jit(solution)/shard_map/all_gather | solution.py:44
  279.7 19.6 %reduce-scatter.8.cloned.1.call-done = f32[8,3072]{1,0:T(8,128)} async-done(((f32[32,3072]{1,0:T(8,128)}), f32[8,3072]{1,0:T(8,128)}) %reduce-scatter.8.cloned.1.call-update) | async-done | bytes 98320 | tf_op jit(solution)/shard_map/reduce_scatter | solution.py:129
  305.8 5.6 all_gather.82
  311.4 5.2 conditional.16
  311.4 5.2 fusion.174
  317.1 5.0 all_gather.84
  323.1 4.5 all_gather.83
  338.3 15.1 %reduce-scatter.10.cloned.1.call-done = f32[8,3072]{1,0:T(8,128)} async-done(((f32[32,3072]{1,0:T(8,128)}), f32[8,3072]{1,0:T(8,128)}) %reduce-scatter.10.cloned.1.call-update) | async-done | bytes 98320 | tf_op jit(solution)/shard_map/reduce_scatter | solution.py:129
  360.6 5.6 all_gather.85
  366.2 5.2 conditional.18
  366.2 5.2 fusion.178
  371.9 4.5 all_gather.87
  377.0 4.5 all_gather.86
  393.2 14.4 %reduce-scatter.12.cloned.1.call-done = f32[8,3072]{1,0:T(8,128)} async-done(((f32[32,3072]{1,0:T(8,128)}), f32[8,3072]{1,0:T(8,128)}) %reduce-scatter.12.cloned.1.call-update) | async-done | bytes 98320 | tf_op jit(solution)/shard_map/reduce_scatter | solution.py:129
  414.2 5.6 all_gather.88
  419.8 5.2 conditional.20
  419.8 5.2 fusion.182
  425.5 4.7 all_gather.90
  431.1 4.5 all_gather.89
  446.2 15.2 %reduce-scatter.14.cloned.1.call-done = f32[8,3072]{1,0:T(8,128)} async-done(((f32[32,3072]{1,0:T(8,128)}), f32[8,3072]{1,0:T(8,128)}) %reduce-scatter.14.cloned.1.call-update) | async-done | bytes 98320 | tf_op jit(solution)/shard_map/reduce_scatter | solution.py:129
  468.0 5.6 all_gather.91
  473.6 5.2 conditional.22
  473.6 5.2 fusion.186
  479.2 4.5 all_gather.93
  484.7 4.5 all_gather.92
  500.1 15.6 %reduce-scatter.16.cloned.1.call-done = f32[8,3072]{1,0:T(8,128)} async-done(((f32[32,3072]{1,0:T(8,128)}), f32[8,3072]{1,0:T(8,128)}) %reduce-scatter.16.cloned.1.call-update) | async-done | bytes 98320 | tf_op jit(solution)/shard_map/reduce_scatter | solution.py:129
  522.2 5.6 all_gather.94
  527.8 5.2 conditional.24
  527.8 5.2 fusion.190
  533.5 4.7 all_gather.96
  539.1 4.5 all_gather.95
  554.6 14.8 %reduce-scatter.18.cloned.1.call-done = f32[8,3072]{1,0:T(8,128)} async-done(((f32[32,3072]{1,0:T(8,128)}), f32[8,3072]{1,0:T(8,128)}) %reduce-scatter.18.cloned.1.call-update) | async-done | bytes 98320 | tf_op jit(solution)/shard_map/reduce_scatter | solution.py:129
  575.9 5.6 all_gather.97
  581.5 5.2 conditional.26
  581.5 5.2 fusion.194
  587.1 4.5 all_gather.99
  603.0 5.0 collective-permute-done.17
  608.0 15.5 %reduce-scatter.20.cloned.1.call-done = f32[8,3072]{1,0:T(8,128)} async-done(((f32[32,3072]{1,0:T(8,128)}), f32[8,3072]{1,0:T(8,128)}) %reduce-scatter.20.cloned.1.call-update) | async-done | bytes 98320 | tf_op jit(solution)/shard_map/reduce_scatter | solution.py:129
  (318 shorter events, 145.9 us)
Async XLA Ops:
  6.5 16.6 %copy-start = (bf16[2,384,1536]{2,1,0:T(8,128)(2,1)S(1)}, bf16[2,384,1536]{2,1,0:T(8,128)(2,1)}, u32[]{:S(2)}) copy-start(bf16[2,384,1536]{2,1,0:T(8,128)(2,1)} %param.42) | copy-start | bytes 7077892
  6.5 102.5 %all-gather.11.cloned.1.call-start = ((), (), s32[]{:S(2)}) async-start(), calls=%async_computation.15 | async-start | bytes 10616832 | tf_op jit(solution)/shard_map/all_gather | solution.py:43
  16.9 182.9 %all-gather.9.cloned.1.call-start = ((), (), s32[]{:S(2)}) async-start(), calls=%async_computation.14 | async-start | bytes 10616832 | tf_op jit(solution)/shard_map/all_gather | solution.py:42
  23.0 1.9 copy-start.9
  23.1 5.4 copy-start.11
  23.1 6.0 copy-start.8
  23.1 214.8 %all-gather.15.cloned.1.call-start = ((), (), s32[]{:S(2)}) async-start(), calls=%async_computation.17 | async-start | bytes 3538944 | tf_op jit(solution)/shard_map/all_gather | solution.py:45
  24.3 251.1 %all-gather.13.cloned.1.call-start = ((), (), s32[]{:S(2)}) async-start(), calls=%async_computation.16 | async-start | bytes 3538944 | tf_op jit(solution)/shard_map/all_gather | solution.py:44
  24.9 274.4 %reduce-scatter.8.cloned.1.call-start = ((), (), s32[]{:S(2)}) async-start(), calls=%async_computation.7 | async-start | bytes 491520 | tf_op jit(solution)/shard_map/reduce_scatter | solution.py:129
  199.8 16.4 %copy-start.19 = (pred[256]{0:T(512)(128)(4,1)S(1)}, pred[256]{0:T(512)(128)(4,1)}, u32[]{:S(2)}) copy-start(pred[256]{0:T(512)(128)(4,1)} %compare_or_fusion) | copy-start | bytes 772
  216.0 63.7 %copy-start.16 = (f32[1,1,2,128]{3,2,1,0:T(2,128)S(1)}, f32[1,1,2,128]{3,2,1,0:T(2,128)}, u32[]{:S(2)}) copy-start(f32[1,1,2,128]{3,2,1,0:T(2,128)} %get-tuple-element.336) | copy-start | bytes 3076
  277.5 0.8 copy-start.1
  278.3 75.1 %reduce-scatter.10.cloned.1.call-start = ((), (), s32[]{:S(2)}) async-start(), calls=%async_computation.8 | async-start | bytes 491520 | tf_op jit(solution)/shard_map/reduce_scatter | solution.py:129
  278.4 25.3 %collective-permute-start = (bf16[8,3072]{1,0:T(8,128)(2,1)S(1)}, bf16[8,3072]{1,0:T(8,128)(2,1)S(1)}, u32[]{:S(2)}, u32[]{:S(2)}) collective-permute-start(bf16[8,3072]{1,0:T(8,128)(2,1)S(1)} %bitcast.470), channel_id=1, source_target_pairs={{8,0},{16,8},{24,16},{9,1},{17,9},{25,17},{10,2},{18,10},{26,18},{... | collective-permute-start | bytes 147464 | tf_op jit(solution)/shard_map/ppermute | solution.py:11
  300.2 5.1 collective-permute-start.6
  311.4 17.3 %copy-start.20 = (pred[256]{0:T(512)(128)(4,1)S(1)}, pred[256]{0:T(512)(128)(4,1)}, u32[]{:S(2)}) copy-start(pred[256]{0:T(512)(128)(4,1)} %compare_or_fusion) | copy-start | bytes 772
  327.8 5.8 copy-start.15
  331.4 0.7 copy-start.2
  332.2 75.5 %reduce-scatter.12.cloned.1.call-start = ((), (), s32[]{:S(2)}) async-start(), calls=%async_computation.9 | async-start | bytes 491520 | tf_op jit(solution)/shard_map/reduce_scatter | solution.py:129
  332.3 6.0 collective-permute-start.12
  334.1 23.6 %collective-permute-start.1 = (bf16[8,3072]{1,0:T(8,128)(2,1)S(1)}, bf16[8,3072]{1,0:T(8,128)(2,1)S(1)}, u32[]{:S(2)}, u32[]{:S(2)}) collective-permute-start(bf16[8,3072]{1,0:T(8,128)(2,1)S(1)} %collective-permute-done), channel_id=1, source_target_pairs={{8,0},{16,8},{24,16},{9,1},{17,9},{25,17},{10,2},{18,10},{26,18},{... | collective-permute-start | bytes 147464 | tf_op jit(solution)/shard_map/ppermute | solution.py:11
  354.3 5.1 collective-permute-start.7
  366.2 15.9 %copy-start.17 = (f32[128]{0:T(128)S(1)}, f32[128]{0:T(128)}, u32[]{:S(2)}) copy-start(f32[128]{0:T(128)} %get-tuple-element.347) | copy-start | bytes 1540
  366.2 16.0 %copy-start.21 = (pred[256]{0:T(512)(128)(4,1)S(1)}, pred[256]{0:T(512)(128)(4,1)}, u32[]{:S(2)}) copy-start(pred[256]{0:T(512)(128)(4,1)} %compare_or_fusion) | copy-start | bytes 772
  381.7 5.4 copy-start.14
  382.5 31.5 %copy-start.10 = (f32[1,1,1,3072]{3,1,2,0:T(1,128)S(1)}, f32[1,1,1,3072]{3,1,2,0:T(1,128)}, u32[]{:S(2)}) copy-start(f32[1,1,1,3072]{3,1,2,0:T(1,128)} %get-tuple-element.326) | copy-start | bytes 36868
  385.7 75.7 %reduce-scatter.14.cloned.1.call-start = ((), (), s32[]{:S(2)}) async-start(), calls=%async_computation.10 | async-start | bytes 491520 | tf_op jit(solution)/shard_map/reduce_scatter | solution.py:129
  385.8 7.5 %collective-permute-start.13 = (bf16[8,3072]{1,0:T(8,128)(2,1)S(1)}, bf16[8,3072]{1,0:T(8,128)(2,1)S(1)}, u32[]{:S(2)}, u32[]{:S(2)}) collective-permute-start(bf16[8,3072]{1,0:T(8,128)(2,1)S(1)} %get-tuple-element.281), channel_id=1, source_target_pairs={{8,0},{16,8},{24,16},{9,1},{17,9},{25,17},{10,2},{18,10},{26,18},{... | collective-permute-start | bytes 147464 | tf_op jit(solution)/shard_map/ppermute | solution.py:11
  387.6 24.4 %collective-permute-start.2 = (bf16[8,3072]{1,0:T(8,128)(2,1)S(1)}, bf16[8,3072]{1,0:T(8,128)(2,1)S(1)}, u32[]{:S(2)}, u32[]{:S(2)}) collective-permute-start(bf16[8,3072]{1,0:T(8,128)(2,1)S(1)} %collective-permute-done.1), channel_id=1, source_target_pairs={{8,0},{16,8},{24,16},{9,1},{17,9},{25,17},{10,2},{18,10},{26,18},{... | collective-permute-start | bytes 147464 | tf_op jit(solution)/shard_map/ppermute | solution.py:11
  408.6 5.1 collective-permute-start.8
  419.8 16.8 %copy-start.18 = (f32[128]{0:T(128)S(1)}, f32[128]{0:T(128)}, u32[]{:S(2)}) copy-start(f32[128]{0:T(128)} %get-tuple-element.345) | copy-start | bytes 1540
  419.8 16.9 %copy-start.22 = (pred[256]{0:T(512)(128)(4,1)S(1)}, pred[256]{0:T(512)(128)(4,1)}, u32[]{:S(2)}) copy-start(pred[256]{0:T(512)(128)(4,1)} %compare_or_fusion) | copy-start | bytes 772
  435.8 5.7 copy-start.13
  440.2 75.5 %reduce-scatter.16.cloned.1.call-start = ((), (), s32[]{:S(2)}) async-start(), calls=%async_computation.11 | async-start | bytes 491520 | tf_op jit(solution)/shard_map/reduce_scatter | solution.py:129
  440.2 6.0 collective-permute-start.14
  441.6 24.3 %collective-permute-start.3 = (bf16[8,3072]{1,0:T(8,128)(2,1)S(1)}, bf16[8,3072]{1,0:T(8,128)(2,1)S(1)}, u32[]{:S(2)}, u32[]{:S(2)}) collective-permute-start(bf16[8,3072]{1,0:T(8,128)(2,1)S(1)} %collective-permute-done.2), channel_id=1, source_target_pairs={{8,0},{16,8},{24,16},{9,1},{17,9},{25,17},{10,2},{18,10},{26,18},{... | collective-permute-start | bytes 147464 | tf_op jit(solution)/shard_map/ppermute | solution.py:11
  462.4 5.1 collective-permute-start.9
  489.4 5.7 copy-start.12
  493.8 75.6 %reduce-scatter.18.cloned.1.call-start = ((), (), s32[]{:S(2)}) async-start(), calls=%async_computation.12 | async-start | bytes 491520 | tf_op jit(solution)/shard_map/reduce_scatter | solution.py:129
  493.8 6.3 collective-permute-start.15
  495.1 24.9 %collective-permute-start.4 = (bf16[8,3072]{1,0:T(8,128)(2,1)S(1)}, bf16[8,3072]{1,0:T(8,128)(2,1)S(1)}, u32[]{:S(2)}, u32[]{:S(2)}) collective-permute-start(bf16[8,3072]{1,0:T(8,128)(2,1)S(1)} %collective-permute-done.3), channel_id=1, source_target_pairs={{8,0},{16,8},{24,16},{9,1},{17,9},{25,17},{10,2},{18,10},{26,18},{... | collective-permute-start | bytes 147464 | tf_op jit(solution)/shard_map/ppermute | solution.py:11
  516.6 5.1 collective-permute-start.10
  548.2 75.3 %reduce-scatter.20.cloned.1.call-start = ((), (), s32[]{:S(2)}) async-start(), calls=%async_computation.13 | async-start | bytes 491520 | tf_op jit(solution)/shard_map/reduce_scatter | solution.py:129
  548.3 6.3 collective-permute-start.16
  549.6 24.1 %collective-permute-start.5 = (bf16[8,3072]{1,0:T(8,128)(2,1)S(1)}, bf16[8,3072]{1,0:T(8,128)(2,1)S(1)}, u32[]{:S(2)}, u32[]{:S(2)}) collective-permute-start(bf16[8,3072]{1,0:T(8,128)(2,1)S(1)} %collective-permute-done.4), channel_id=1, source_target_pairs={{8,0},{16,8},{24,16},{9,1},{17,9},{25,17},{10,2},{18,10},{26,18},{... | collective-permute-start | bytes 147464 | tf_op jit(solution)/shard_map/ppermute | solution.py:11
  570.3 5.1 collective-permute-start.11
  600.9 0.8 copy-start.7
  601.7 6.3 collective-permute-start.17
  (4 other events, 3.0 us)
Sparse Core Ops, SparseCore 0:
  17.0 91.9 all-gather.10
  110.5 89.2 all-gather.8
  201.4 36.4 all-gather.14
  239.2 36.0 all-gather.12
  278.4 20.8 reduce-scatter.7
  332.3 20.9 reduce-scatter.9
  385.8 21.7 reduce-scatter.11
  440.3 21.1 reduce-scatter.13
  493.9 21.7 reduce-scatter.15
  548.3 20.9 reduce-scatter.17
  601.8 21.6 reduce-scatter.19
where the time goes:
time: 641 us; the launch traced here: 632 us
  waiting for transfers between devices  366 us (57%)
  blocking collectives  105 us (16%)
  matrix products  55.1 us (9%)
  local copies, waits for them, and re-layouts  38 us (6%)
  starting transfers between devices  36.3 us (6%)
  other arithmetic  16 us (2%)
  between operations  15.7 us (2%)
    reduce_scatter x7, waiting for transfers between devices, local(): lax.psum_scatter(partial_value, 'uly', scatter_dimension=0, tiled=True)  110 us
    all_gather x1, waiting for transfers between devices, local(): lax.all_gather(qkv_video[0], 'blk', axis=0, tiled=True)  90.8 us
    all_gather x1, waiting for transfers between devices, local(): lax.all_gather(text_rows_w, 'blk', axis=0, tiled=True)  72.1 us
    all_gather x7, blocking collectives, local(): gathered = lax.all_gather(modded, 'uly', axis=0, tiled=True)  40.5 us
    all_gather x1, waiting for transfers between devices, local(): lax.all_gather(out_video[0], 'blk', axis=1, tiled=True)  37.5 us
    ppermute x18, starting transfers between devices, from_behind(): return lax.ppermute(shard, axis, pairs)  35.8 us
    ppermute x18, waiting for transfers between devices, from_behind(): return lax.ppermute(shard, axis, pairs)  33.3 us
    all_gather x7, blocking collectives, local(): lax.all_gather(fresh_keys, 'blk', axis=0, tiled=True)  32.4 us
  transfers between devices with their start and end apart: 29, of which 23 were waited for; matrix products, arithmetic and copies ran while one was open for 4% of the time, Pallas kernels for 0%

commit v1 on v0

--- a/solution.py
+++ b/solution.py
@@ -3,6 +3,28 @@
 import jax.numpy as jnp
 from jax import lax
 from jax.sharding import PartitionSpec as P
+
+
+def _perform_scales(vec, d0):
+    z1 = list(vec.shape[1:])
+    z1[d0] *= vec.shape[0]
+    return jnp.moveaxis(vec, 0, d0).reshape(z1)
+
+
+def _do_vectors(xin, mesh_name):
+    x_now, later = (lax.axis_size(mesh_name), lax.axis_index(mesh_name))
+    y_new, frame_out = (xin[None], 1)
+    while frame_out < x_now:
+        copies = []
+        for j in tuple(range(x_now)):
+            copies.append((j, j ^ frame_out))
+        local_out = lax.ppermute(y_new, mesh_name, copies)
+        main = later & frame_out == 0
+        y_new = jnp.concatenate(
+            [jnp.where(main, y_new, local_out), jnp.where(main, local_out, y_new)]
+        )
+        frame_out *= 2
+    return y_new
 
 
 def from_behind(shard, axis, by):
@@ -38,10 +60,14 @@
     chosen = jnp.minimum(section, dual_count - 1)
     text_rows_w = lax.dynamic_index_in_dim(qkv_text, chosen, 0, keepdims=False)
     text_cols_w = lax.dynamic_index_in_dim(out_text, chosen, 0, keepdims=False)
+
+    def columns_remake(v0, packet, array_dim):
+        return _perform_scales(_do_vectors(packet, v0), array_dim)
+
     video_proj, text_proj, video_back, text_back = (
         lax.all_gather(qkv_video[0], "blk", axis=0, tiled=True),
         lax.all_gather(text_rows_w, "blk", axis=0, tiled=True),
-        lax.all_gather(out_video[0], "blk", axis=1, tiled=True),
+        columns_remake("blk", out_video[0], 1),
         lax.all_gather(text_cols_w, "blk", axis=1, tiled=True),
     )
     video_proj = video_proj.reshape(width, 3 * local_width)

time: 641 us -> 617 us (0.963)
  waiting for transfers between devices: 366 us -> 343 us
  matrix products: 55.1 us -> 47.7 us
    all_gather x1 -> x0, waiting for transfers between devices: 37.5 us -> none  [local(): lax.all_gather(out_video[0], 'blk', axis=1, tiled=True)]
    ppermute x0 -> x1, waiting for transfers between devices: none -> 36 us  [_do_vectors(): local_out = lax.ppermute(y_new, mesh_name, copies)]
    all_gather x1, waiting for transfers between devices: 72.1 us -> 52.6 us  [local(): lax.all_gather(text_rows_w, 'blk', axis=0, tiled=True)]
    dot_general x6, matrix products: 13.1 us -> 4.95 us  [local(): jnp.dot(operand, video_back, preferred_element_type=jnp.float32)]
    unnamed x57 -> x59, local copies, waits for them, and re-layouts: 17.8 us -> 17.9 us
  transfers between devices with their start and end apart: 29 -> 29, of which waited for: 23 -> 23; matrix products, arithmetic and copies ran while one was open for 4% -> 5% of each run, Pallas kernels for 0% -> 0%
where the time goes in v1:
time: 617 us; the launch traced here: 607 us
  waiting for transfers between devices  343 us (56%)
  blocking collectives  104 us (17%)
  matrix products  47.7 us (8%)
  starting transfers between devices  39.2 us (6%)
  local copies, waits for them, and re-layouts  38.4 us (6%)
  other arithmetic  18.7 us (3%)
  between operations  16 us (3%)
    reduce_scatter x7, waiting for transfers between devices, local(): lax.psum_scatter(partial_value, 'uly', scatter_dimension=0, tiled=True)  107 us
    all_gather x1, waiting for transfers between devices, local(): lax.all_gather(qkv_video[0], 'blk', axis=0, tiled=True)  92.3 us
    all_gather x1, waiting for transfers between devices, local(): lax.all_gather(text_rows_w, 'blk', axis=0, tiled=True)  52.6 us
    all_gather x7, blocking collectives, local(): gathered = lax.all_gather(modded, 'uly', axis=0, tiled=True)  39.2 us
    ppermute x1, waiting for transfers between devices, _do_vectors(): local_out = lax.ppermute(y_new, mesh_name, copies)  36 us
    ppermute x18, starting transfers between devices, from_behind(): return lax.ppermute(shard, axis, pairs)  35.8 us
    ppermute x18, waiting for transfers between devices, from_behind(): return lax.ppermute(shard, axis, pairs)  34.8 us
    all_gather x7, blocking collectives, local(): lax.all_gather(fresh_keys, 'blk', axis=0, tiled=True)  32.4 us
  transfers between devices with their start and end apart: 29, of which 23 were waited for; matrix products, arithmetic and copies ran while one was open for 5% of the time, Pallas kernels for 0%

profile of v1, /device:TPU:0, one launch (start us, length us, event | category | flops | bytes accessed | tf_op | source)
XLA Modules:
  0.0 606.6 jit_solution(3050480046043558497)
XLA Ops:
  10.8 6.1 %copy.202 = bf16[1,1536,3,384]{1,3,2,0:T(8,128)(2,1)} copy(bf16[1,1536,3,384]{3,1,2,0:T(8,128)(2,1)} %constant_dynamic-slice_fusion.23) | data formatting | bytes 7077888
  16.9 6.1 %copy.111 = bf16[1,1536,3,384]{1,3,2,0:T(8,128)(2,1)} copy(bf16[1,1536,3,384]{3,1,2,0:T(8,128)(2,1)} %param.39) | data formatting | bytes 7077888 | tf_op args[2]
  30.2 5.6 all_gather.72
  37.6 36.0 %collective-permute-done.6 = bf16[1,384,1536]{2,1,0:T(8,128)(2,1)} collective-permute-done((bf16[1,384,1536]{2,1,0:T(8,128)(2,1)}, bf16[1,384,1536]{2,1,0:T(8,128)(2,1)}, u32[]{:S(2)}, u32[]{:S(2)}) %collective-permute-start.6) | collective-permute-done | bytes 1179680 | tf_op jit(solution)/shard_map/ppermute | solution.py:21
  75.8 52.6 %all-gather.9.cloned.1.call-done = bf16[1,3072,3,384]{1,3,2,0:T(8,128)(2,1)} async-done(((bf16[1,1536,3,384]{1,3,2,0:T(8,128)(2,1)}), bf16[1,3072,3,384]{1,3,2,0:T(8,128)(2,1)}) %all-gather.9.cloned.1.call-update) | async-done | bytes 7077904 | tf_op jit(solution)/shard_map/all_gather | solution.py:69
  128.4 92.3 %all-gather.7.cloned.1.call-done = bf16[1,3072,3,384]{1,3,2,0:T(8,128)(2,1)} async-done(((bf16[1,1536,3,384]{1,3,2,0:T(8,128)(2,1)}), bf16[1,3072,3,384]{1,3,2,0:T(8,128)(2,1)}) %all-gather.7.cloned.1.call-update) | async-done | bytes 7077904 | tf_op jit(solution)/shard_map/all_gather | solution.py:68
  220.7 5.2 conditional.14
  220.7 5.2 fusion.171
  226.3 4.5 all_gather.76
  230.8 5.0 all_gather.75
  239.0 19.7 %all-gather.11.cloned.1.call-done = bf16[1,384,3072]{2,1,0:T(8,128)(2,1)} async-done(((bf16[1,384,1536]{2,1,0:T(8,128)(2,1)}), bf16[1,384,3072]{2,1,0:T(8,128)(2,1)}) %all-gather.11.cloned.1.call-update) | async-done | bytes 2359312 | tf_op jit(solution)/shard_map/all_gather | solution.py:71
  263.7 18.3 %reduce-scatter.8.cloned.1.call-done = f32[8,3072]{1,0:T(8,128)} async-done(((f32[32,3072]{1,0:T(8,128)}), f32[8,3072]{1,0:T(8,128)}) %reduce-scatter.8.cloned.1.call-update) | async-done | bytes 98320 | tf_op jit(solution)/shard_map/reduce_scatter | solution.py:155
  288.5 5.6 all_gather.78
  294.1 5.2 conditional.16
  294.1 5.2 fusion.174
  299.7 5.0 all_gather.80
  305.7 4.5 all_gather.79
  320.9 13.4 %reduce-scatter.10.cloned.1.call-done = f32[8,3072]{1,0:T(8,128)} async-done(((f32[32,3072]{1,0:T(8,128)}), f32[8,3072]{1,0:T(8,128)}) %reduce-scatter.10.cloned.1.call-update) | async-done | bytes 98320 | tf_op jit(solution)/shard_map/reduce_scatter | solution.py:155
  341.6 5.6 all_gather.81
  347.2 5.2 conditional.18
  347.2 5.2 fusion.178
  352.9 4.5 all_gather.83
  358.0 4.5 all_gather.82
  372.6 14.4 %reduce-scatter.12.cloned.1.call-done = f32[8,3072]{1,0:T(8,128)} async-done(((f32[32,3072]{1,0:T(8,128)}), f32[8,3072]{1,0:T(8,128)}) %reduce-scatter.12.cloned.1.call-update) | async-done | bytes 98320 | tf_op jit(solution)/shard_map/reduce_scatter | solution.py:155
  393.5 5.6 all_gather.84
  399.2 5.2 conditional.20
  399.2 5.2 fusion.182
  404.8 4.7 all_gather.86
  410.4 4.5 all_gather.85
  423.9 15.2 %reduce-scatter.14.cloned.1.call-done = f32[8,3072]{1,0:T(8,128)} async-done(((f32[32,3072]{1,0:T(8,128)}), f32[8,3072]{1,0:T(8,128)}) %reduce-scatter.14.cloned.1.call-update) | async-done | bytes 98320 | tf_op jit(solution)/shard_map/reduce_scatter | solution.py:155
  445.6 5.6 all_gather.87
  451.3 5.2 conditional.22
  451.3 5.2 fusion.186
  456.9 4.5 all_gather.89
  462.4 4.5 all_gather.88
  476.1 15.6 %reduce-scatter.16.cloned.1.call-done = f32[8,3072]{1,0:T(8,128)} async-done(((f32[32,3072]{1,0:T(8,128)}), f32[8,3072]{1,0:T(8,128)}) %reduce-scatter.16.cloned.1.call-update) | async-done | bytes 98320 | tf_op jit(solution)/shard_map/reduce_scatter | solution.py:155
  498.2 5.6 all_gather.90
  503.8 5.2 conditional.24
  503.8 5.2 fusion.190
  509.5 4.7 all_gather.92
  515.2 4.5 all_gather.91
  528.9 14.8 %reduce-scatter.18.cloned.1.call-done = f32[8,3072]{1,0:T(8,128)} async-done(((f32[32,3072]{1,0:T(8,128)}), f32[8,3072]{1,0:T(8,128)}) %reduce-scatter.18.cloned.1.call-update) | async-done | bytes 98320 | tf_op jit(solution)/shard_map/reduce_scatter | solution.py:155
  550.2 5.6 all_gather.93
  555.8 5.2 conditional.26
  555.8 5.2 fusion.194
  561.5 4.5 all_gather.95
  577.5 5.0 collective-permute-done.18
  582.5 15.5 %reduce-scatter.20.cloned.1.call-done = f32[8,3072]{1,0:T(8,128)} async-done(((f32[32,3072]{1,0:T(8,128)}), f32[8,3072]{1,0:T(8,128)}) %reduce-scatter.20.cloned.1.call-update) | async-done | bytes 98320 | tf_op jit(solution)/shard_map/reduce_scatter | solution.py:155
  (322 shorter events, 137.4 us)
Async XLA Ops:
  6.5 19.6 %copy-start = (bf16[2,384,1536]{2,1,0:T(8,128)(2,1)S(1)}, bf16[2,384,1536]{2,1,0:T(8,128)(2,1)}, u32[]{:S(2)}) copy-start(bf16[2,384,1536]{2,1,0:T(8,128)(2,1)} %param.42) | copy-start | bytes 7077892
  6.5 121.9 %all-gather.9.cloned.1.call-start = ((), (), s32[]{:S(2)}) async-start(), calls=%async_computation.15 | async-start | bytes 10616832 | tf_op jit(solution)/shard_map/all_gather | solution.py:69
  16.9 203.8 %all-gather.7.cloned.1.call-start = ((), (), s32[]{:S(2)}) async-start(), calls=%async_computation.14 | async-start | bytes 10616832 | tf_op jit(solution)/shard_map/all_gather | solution.py:68
  23.1 4.3 copy-start.11
  23.1 4.7 copy-start.12
  23.1 235.7 %all-gather.11.cloned.1.call-start = ((), (), s32[]{:S(2)}) async-start(), calls=%async_computation.16 | async-start | bytes 3538944 | tf_op jit(solution)/shard_map/all_gather | solution.py:71
  23.1 50.4 %collective-permute-start.6 = (bf16[1,384,1536]{2,1,0:T(8,128)(2,1)}, bf16[1,384,1536]{2,1,0:T(8,128)(2,1)}, u32[]{:S(2)}, u32[]{:S(2)}) collective-permute-start(bf16[1,384,1536]{2,1,0:T(8,128)(2,1)} %param.41), channel_id=1, source_target_pairs={{0,4},{4,0},{1,5},{5,1},{2,6},{6,2},{3,7},{7,3},{8,12},{12,8},{9,1... | collective-permute-start | bytes 3538952 | tf_op jit(solution)/shard_map/ppermute | solution.py:21
  27.2 2.0 copy-start.10
  27.2 9.2 %copy-start.14 = (f32[1,2,2,128]{3,2,1,0:T(2,128)S(1)}, f32[1,2,2,128]{3,2,1,0:T(2,128)}, u32[]{:S(2)}) copy-start(f32[1,2,2,128]{3,2,1,0:T(2,128)} %param.44) | copy-start | bytes 6148
  27.3 254.7 %reduce-scatter.8.cloned.1.call-start = ((), (), s32[]{:S(2)}) async-start(), calls=%async_computation.7 | async-start | bytes 491520 | tf_op jit(solution)/shard_map/reduce_scatter | solution.py:155
  75.8 445.4 %copy-start.2 = (bf16[2,48,8,1536]{3,2,0,1:T(8,128)(2,1)}, bf16[2,48,8,1536]{3,2,0,1:T(8,128)(2,1)S(1)}, u32[]{:S(2)}) copy-start(bf16[2,48,8,1536]{3,2,0,1:T(8,128)(2,1)S(1)} %copy.205) | copy-start | bytes 7077892
  260.9 0.8 copy-start.3
  261.7 72.7 %reduce-scatter.10.cloned.1.call-start = ((), (), s32[]{:S(2)}) async-start(), calls=%async_computation.8 | async-start | bytes 491520 | tf_op jit(solution)/shard_map/reduce_scatter | solution.py:155
  261.8 24.5 %collective-permute-start = (bf16[8,3072]{1,0:T(8,128)(2,1)S(1)}, bf16[8,3072]{1,0:T(8,128)(2,1)S(1)}, u32[]{:S(2)}, u32[]{:S(2)}) collective-permute-start(bf16[8,3072]{1,0:T(8,128)(2,1)S(1)} %bitcast.473), channel_id=1, source_target_pairs={{8,0},{16,8},{24,16},{9,1},{17,9},{25,17},{10,2},{18,10},{26,18},{... | collective-permute-start | bytes 147464 | tf_op jit(solution)/shard_map/ppermute | solution.py:33
  282.9 5.1 collective-permute-start.7
  299.2 12.0 %copy-start.20 = (f32[128]{0:T(128)S(1)}, f32[128]{0:T(128)}, u32[]{:S(2)}) copy-start(f32[128]{0:T(128)} %get-tuple-element.351) | copy-start | bytes 1540
  299.2 12.1 %copy-start.21 = (pred[256]{0:T(512)(128)(4,1)S(1)}, pred[256]{0:T(512)(128)(4,1)}, u32[]{:S(2)}) copy-start(pred[256]{0:T(512)(128)(4,1)} %compare_or_fusion) | copy-start | bytes 772
  313.2 73.8 %reduce-scatter.12.cloned.1.call-start = ((), (), s32[]{:S(2)}) async-start(), calls=%async_computation.9 | async-start | bytes 491520 | tf_op jit(solution)/shard_map/reduce_scatter | solution.py:155
  313.3 7.7 %collective-permute-start.13 = (bf16[8,3072]{1,0:T(8,128)(2,1)S(1)}, bf16[8,3072]{1,0:T(8,128)(2,1)S(1)}, u32[]{:S(2)}, u32[]{:S(2)}) collective-permute-start(bf16[8,3072]{1,0:T(8,128)(2,1)S(1)} %get-tuple-element.283), channel_id=1, source_target_pairs={{8,0},{16,8},{24,16},{9,1},{17,9},{25,17},{10,2},{18,10},{26,18},{... | collective-permute-start | bytes 147464 | tf_op jit(solution)/shard_map/ppermute | solution.py:33
  315.2 23.6 %collective-permute-start.1 = (bf16[8,3072]{1,0:T(8,128)(2,1)S(1)}, bf16[8,3072]{1,0:T(8,128)(2,1)S(1)}, u32[]{:S(2)}, u32[]{:S(2)}) collective-permute-start(bf16[8,3072]{1,0:T(8,128)(2,1)S(1)} %collective-permute-done), channel_id=1, source_target_pairs={{8,0},{16,8},{24,16},{9,1},{17,9},{25,17},{10,2},{18,10},{26,18},{... | collective-permute-start | bytes 147464 | tf_op jit(solution)/shard_map/ppermute | solution.py:33
  335.3 5.1 collective-permute-start.8
  352.4 10.7 %copy-start.18 = (f32[128]{0:T(128)S(1)}, f32[128]{0:T(128)}, u32[]{:S(2)}) copy-start(f32[128]{0:T(128)} %get-tuple-element.349) | copy-start | bytes 1540
  352.4 10.8 %copy-start.22 = (pred[256]{0:T(512)(128)(4,1)S(1)}, pred[256]{0:T(512)(128)(4,1)}, u32[]{:S(2)}) copy-start(pred[256]{0:T(512)(128)(4,1)} %compare_or_fusion) | copy-start | bytes 772
  363.8 2.7 copy-start.17
  363.8 29.7 %copy-start.13 = (f32[1,1,1,3072]{3,1,2,0:T(1,128)S(1)}, f32[1,1,1,3072]{3,1,2,0:T(1,128)}, u32[]{:S(2)}) copy-start(f32[1,1,1,3072]{3,1,2,0:T(1,128)} %get-tuple-element.328) | copy-start | bytes 36868
  365.1 74.0 %reduce-scatter.14.cloned.1.call-start = ((), (), s32[]{:S(2)}) async-start(), calls=%async_computation.10 | async-start | bytes 491520 | tf_op jit(solution)/shard_map/reduce_scatter | solution.py:155
  365.1 7.5 %collective-permute-start.14 = (bf16[8,3072]{1,0:T(8,128)(2,1)S(1)}, bf16[8,3072]{1,0:T(8,128)(2,1)S(1)}, u32[]{:S(2)}, u32[]{:S(2)}) collective-permute-start(bf16[8,3072]{1,0:T(8,128)(2,1)S(1)} %get-tuple-element.281), channel_id=1, source_target_pairs={{8,0},{16,8},{24,16},{9,1},{17,9},{25,17},{10,2},{18,10},{26,18},{... | collective-permute-start | bytes 147464 | tf_op jit(solution)/shard_map/ppermute | solution.py:33
  367.0 24.4 %collective-permute-start.2 = (bf16[8,3072]{1,0:T(8,128)(2,1)S(1)}, bf16[8,3072]{1,0:T(8,128)(2,1)S(1)}, u32[]{:S(2)}, u32[]{:S(2)}) collective-permute-start(bf16[8,3072]{1,0:T(8,128)(2,1)S(1)} %collective-permute-done.1), channel_id=1, source_target_pairs={{8,0},{16,8},{24,16},{9,1},{17,9},{25,17},{10,2},{18,10},{26,18},{... | collective-permute-start | bytes 147464 | tf_op jit(solution)/shard_map/ppermute | solution.py:33
  387.9 5.1 collective-permute-start.9
  404.3 11.6 %copy-start.19 = (f32[128]{0:T(128)S(1)}, f32[128]{0:T(128)}, u32[]{:S(2)}) copy-start(f32[128]{0:T(128)} %get-tuple-element.347) | copy-start | bytes 1540
  404.3 11.7 %copy-start.23 = (pred[256]{0:T(512)(128)(4,1)S(1)}, pred[256]{0:T(512)(128)(4,1)}, u32[]{:S(2)}) copy-start(pred[256]{0:T(512)(128)(4,1)} %compare_or_fusion) | copy-start | bytes 772
  416.6 2.7 copy-start.16
  417.9 73.8 %reduce-scatter.16.cloned.1.call-start = ((), (), s32[]{:S(2)}) async-start(), calls=%async_computation.11 | async-start | bytes 491520 | tf_op jit(solution)/shard_map/reduce_scatter | solution.py:155
  417.9 6.0 collective-permute-start.15
  419.2 24.2 %collective-permute-start.3 = (bf16[8,3072]{1,0:T(8,128)(2,1)S(1)}, bf16[8,3072]{1,0:T(8,128)(2,1)S(1)}, u32[]{:S(2)}, u32[]{:S(2)}) collective-permute-start(bf16[8,3072]{1,0:T(8,128)(2,1)S(1)} %collective-permute-done.2), channel_id=1, source_target_pairs={{8,0},{16,8},{24,16},{9,1},{17,9},{25,17},{10,2},{18,10},{26,18},{... | collective-permute-start | bytes 147464 | tf_op jit(solution)/shard_map/ppermute | solution.py:33
  440.0 5.1 collective-permute-start.10
  468.5 2.7 copy-start.15
  469.8 73.9 %reduce-scatter.18.cloned.1.call-start = ((), (), s32[]{:S(2)}) async-start(), calls=%async_computation.12 | async-start | bytes 491520 | tf_op jit(solution)/shard_map/reduce_scatter | solution.py:155
  469.8 6.3 %collective-permute-start.16 = (bf16[8,3072]{1,0:T(8,128)(2,1)S(1)}, bf16[8,3072]{1,0:T(8,128)(2,1)S(1)}, u32[]{:S(2)}, u32[]{:S(2)}) collective-permute-start(bf16[8,3072]{1,0:T(8,128)(2,1)S(1)} %get-tuple-element.277), channel_id=1, source_target_pairs={{8,0},{16,8},{24,16},{9,1},{17,9},{25,17},{10,2},{18,10},{26,18},{... | collective-permute-start | bytes 147464 | tf_op jit(solution)/shard_map/ppermute | solution.py:33
  471.1 24.9 %collective-permute-start.4 = (bf16[8,3072]{1,0:T(8,128)(2,1)S(1)}, bf16[8,3072]{1,0:T(8,128)(2,1)S(1)}, u32[]{:S(2)}, u32[]{:S(2)}) collective-permute-start(bf16[8,3072]{1,0:T(8,128)(2,1)S(1)} %collective-permute-done.3), channel_id=1, source_target_pairs={{8,0},{16,8},{24,16},{9,1},{17,9},{25,17},{10,2},{18,10},{26,18},{... | collective-permute-start | bytes 147464 | tf_op jit(solution)/shard_map/ppermute | solution.py:33
  492.6 5.1 collective-permute-start.11
  522.6 75.4 %reduce-scatter.20.cloned.1.call-start = ((), (), s32[]{:S(2)}) async-start(), calls=%async_computation.13 | async-start | bytes 491520 | tf_op jit(solution)/shard_map/reduce_scatter | solution.py:155
  522.6 6.3 %collective-permute-start.17 = (bf16[8,3072]{1,0:T(8,128)(2,1)S(1)}, bf16[8,3072]{1,0:T(8,128)(2,1)S(1)}, u32[]{:S(2)}, u32[]{:S(2)}) collective-permute-start(bf16[8,3072]{1,0:T(8,128)(2,1)S(1)} %get-tuple-element.275), channel_id=1, source_target_pairs={{8,0},{16,8},{24,16},{9,1},{17,9},{25,17},{10,2},{18,10},{26,18},{... | collective-permute-start | bytes 147464 | tf_op jit(solution)/shard_map/ppermute | solution.py:33
  523.9 24.1 %collective-permute-start.5 = (bf16[8,3072]{1,0:T(8,128)(2,1)S(1)}, bf16[8,3072]{1,0:T(8,128)(2,1)S(1)}, u32[]{:S(2)}, u32[]{:S(2)}) collective-permute-start(bf16[8,3072]{1,0:T(8,128)(2,1)S(1)} %collective-permute-done.4), channel_id=1, source_target_pairs={{8,0},{16,8},{24,16},{9,1},{17,9},{25,17},{10,2},{18,10},{26,18},{... | collective-permute-start | bytes 147464 | tf_op jit(solution)/shard_map/ppermute | solution.py:33
  544.6 5.1 collective-permute-start.12
  573.0 26.5 %copy-start.1 = (bf16[2,384,1536]{2,1,0:T(8,128)(2,1)S(1)}, bf16[2,384,1536]{2,1,0:T(8,128)(2,1)}, u32[]{:S(2)}) copy-start(bf16[2,384,1536]{2,1,0:T(8,128)(2,1)} %param.42) | copy-start | bytes 7077892
  575.4 0.8 copy-start.9
  576.1 6.3 %collective-permute-start.18 = (bf16[8,3072]{1,0:T(8,128)(2,1)S(1)}, bf16[8,3072]{1,0:T(8,128)(2,1)S(1)}, u32[]{:S(2)}, u32[]{:S(2)}) collective-permute-start(bf16[8,3072]{1,0:T(8,128)(2,1)S(1)} %get-tuple-element.273), channel_id=1, source_target_pairs={{8,0},{16,8},{24,16},{9,1},{17,9},{25,17},{10,2},{18,10},{26,18},{... | collective-permute-start | bytes 147464 | tf_op jit(solution)/shard_map/ppermute | solution.py:33
  (5 other events, 3.7 us)
Sparse Core Ops, SparseCore 0:
  17.0 111.3 all-gather.8
  129.9 90.7 all-gather.6
  222.3 36.4 all-gather.10
  261.8 20.0 reduce-scatter.7
  313.3 20.9 reduce-scatter.9
  365.2 21.7 reduce-scatter.11
  418.0 21.0 reduce-scatter.13
  469.9 21.7 reduce-scatter.15
  522.7 20.9 reduce-scatter.17
  576.3 21.6 reduce-scatter.19
